TPU v7x, 32 devices: a whole 2x2x4 slice. The times are simulated.
32 devices in a mesh: groups: 2 (over y), tensor: 4 (over z), dp: 4 (over x, core).
Axes of the slice: x: 2, y: 2, z: 4, core: 2. Of those that a mesh axis runs over, the one named last changes fastest.
Arguments:
- acts: bfloat16 [8, 288, 4096], P(('groups', 'dp')), parts along dimension 0, may hold values from -6 to 6
- out_grads: bfloat16 [8, 288, 14336], P(('groups', 'dp'), None, 'tensor'), parts along dimension 0, may hold values from -0.29882812 to 0.29882812
- basis_in: bfloat16 [8192, 4096], P(('groups', 'dp'), 'tensor'), parts along dimension 0, may hold values from -0.09375 to 0.09375
- basis_out: bfloat16 [28672, 14336], P(('groups', 'dp'), 'tensor'), parts along dimension 0, may hold values from -0.046875 to 0.046875
- lengths: int32 [8], P(('groups', 'dp')), parts along dimension 0, may hold values from 96 to 288
Outputs:
- corrections: bfloat16 [28672, 4096], P(('groups', 'tensor'), 'dp'), parts along dimension 0
There are 2 independent parts, one for each index of `groups`. A program takes and returns all parts, laid end to end along the dimension named above; each array names one. Nothing has to cross between parts.
All inputs are finite; a program needn't handle non-finite values.
Results may differ from a plain program's by a relative error of at most 0.0085.
Values may be sent and summed in bfloat16 or wider, within the bound.
No kernel may reach another device: no remote copies, remote signals or barrier semaphores. Data moves between devices by JAX's collectives and lax.ppermute only.
A program may use at most 320 MiB of HBM per device.

v0:
```python
import jax
import jax.numpy as jnp
from jax import lax
from jax.sharding import PartitionSpec as P


def per_device(acts, out_grads, basis_in, basis_out, lengths):
    seq_len = acts.shape[1]
    keep = (jnp.arange(seq_len, dtype=jnp.int32)[None, :] < lengths[:, None]).astype(acts.dtype)
    kept = acts * keep[:, :, None]
    in_cols = lax.all_gather(basis_in, "dp", axis=0, tiled=True)
    in_local = jnp.einsum("nsd,de->nse", kept, in_cols, preferred_element_type=jnp.float32).astype(
        jnp.bfloat16
    )
    whole = lax.all_gather(out_grads, "tensor", axis=2, tiled=True)
    out_proj = jnp.einsum(
        "nsh,hc->nsc",
        whole,
        lax.all_gather(basis_out, "dp", axis=0, tiled=True),
        preferred_element_type=jnp.float32,
    )
    out_proj = out_proj.astype(jnp.bfloat16)
    in_proj = lax.all_gather(in_local, "tensor", axis=2, tiled=True)
    proj = jnp.einsum("nsc,nse->nce", out_proj, in_proj, preferred_element_type=jnp.float32)
    squares = jnp.sum(proj * proj, axis=0)
    summed = lax.psum_scatter(squares.astype(jnp.bfloat16), "dp", scatter_dimension=1, tiled=True)
    return summed


def solution(mesh):
    in_specs = (
        P(("groups", "dp"), None, None),
        P(("groups", "dp"), None, "tensor"),
        P(("groups", "dp"), "tensor"),
        P(("groups", "dp"), "tensor"),
        P(("groups", "dp")),
    )
    out_specs = P(("groups", "tensor"), "dp")
    return jax.shard_map(
        per_device, mesh=mesh, in_specs=in_specs, out_specs=out_specs, check_vma=False
    )
```

profile of v0, /device:TPU:3, one launch (start us, length us, event | category | flops | bytes accessed | tf_op | source)
XLA Modules:
  0.0 1100.5 jit_solution(9293996275985011838)
XLA Ops:
  6.5 0.0 all-gather.10.cloned.1.call-start
  6.5 0.7 all-gather.10.cloned.1.call-update
  7.3 0.0 all-gather.6.cloned.1.call-start
  7.3 0.7 all-gather.6.cloned.1.call-update
  8.0 0.0 copy-start
  8.0 0.0 all-gather.8.cloned.1.call-start
  8.1 0.7 all-gather.8.cloned.1.call-update
  8.8 0.0 all-gather.12.cloned.1.call-start
  9.5 58.3 %all-gather.10.cloned.1.call-done = bf16[4096,1024]{1,0:T(8,128)(2,1)} async-done(((bf16[1024,1024]{1,0:T(8,128)(2,1)}), bf16[4096,1024]{1,0:T(8,128)(2,1)}) %all-gather.10.cloned.1.call-update) | async-done | bytes 8388624 | tf_op jit(solution)/shard_map/all_gather | solution.py:11
  67.7 0.0 copy-done
  67.7 6.8 fusion.8
  74.6 0.0 all-gather.12.cloned.1.call-update
  74.6 0.0 reduce-scatter.2.cloned.1.call-start
  74.7 143.1 %all-gather.6.cloned.1.call-done = bf16[1,288,14336]{2,1,0:T(8,128)(2,1)} async-done(((bf16[1,288,3584]{2,1,0:T(8,128)(2,1)}), bf16[1,288,14336]{2,1,0:T(8,128)(2,1)}) %all-gather.6.cloned.1.call-update) | async-done | bytes 8257552 | tf_op jit(solution)/shard_map/all_gather | solution.py:15
  217.8 596.9 %all-gather.8.cloned.1.call-done = bf16[14336,3584]{1,0:T(8,128)(2,1)} async-done(((bf16[3584,3584]{1,0:T(8,128)(2,1)}), bf16[14336,3584]{1,0:T(8,128)(2,1)}) %all-gather.8.cloned.1.call-update) | async-done | bytes 102760464 | tf_op jit(solution)/shard_map/all_gather | solution.py:19
  814.7 42.2 %fusion.2 = bf16[288,3584]{1,0:T(8,128)(2,1)S(1)} fusion(bf16[14336,3584]{1,0:T(8,128)(2,1)} %all-gather.8.cloned.1.call-done, bf16[1,288,14336]{2,1,0:T(8,128)(2,1)} %all-gather.6.cloned.1.call-done), kind=kOutput, calls=%fused_computation.3 | convolution fusion | flops 29596041216 | bytes 113082368 | tf_op jit(solution)/shard_map/nsh,hc->nsc/dot_general | solution.py:16
  856.9 10.4 all-gather.12.cloned.1.call-done
  867.3 20.8 %multiply_convert_fusion = bf16[3584,4096]{1,0:T(8,128)(2,1)} fusion(bf16[288,3584]{1,0:T(8,128)(2,1)S(1)} %fusion.2, bf16[288,4096]{1,0:T(8,128)(2,1)} %all-gather.12.cloned.1.call-done), kind=kOutput, calls=%fused_computation | convolution fusion | flops 8485076992 | bytes 33783808 | tf_op jit(solution)/shard_map/nsc,nse->nce/dot_general | solution.py:24
  888.1 0.0 reduce-scatter.2.cloned.1.call-update
  888.1 205.9 %reduce-scatter.2.cloned.1.call-done = bf16[3584,1024]{1,0:T(8,128)(2,1)} async-done(((bf16[3584,4096]{1,0:T(8,128)(2,1)}), bf16[3584,1024]{1,0:T(8,128)(2,1)}) %reduce-scatter.2.cloned.1.call-update) | async-done | bytes 7340048 | tf_op jit(solution)/shard_map/reduce_scatter | solution.py:26
  (1 shorter events, 0.0 us)
Async XLA Ops:
  6.5 61.2 %all-gather.10.cloned.1.call-start = ((), (), s32[]{:S(2)}) async-start(), calls=%async_computation.3 | async-start | bytes 10485760 | tf_op jit(solution)/shard_map/all_gather | solution.py:11
  7.3 210.5 %all-gather.6.cloned.1.call-start = ((), (), s32[]{:S(2)}) async-start(), calls=%async_computation.1 | async-start | bytes 10321920 | tf_op jit(solution)/shard_map/all_gather | solution.py:15
  8.0 59.7 %copy-start = (bf16[1,288,4096]{2,1,0:T(8,128)(2,1)S(1)}, bf16[1,288,4096]{2,1,0:T(8,128)(2,1)}, u32[]{:S(2)}) copy-start(bf16[1,288,4096]{2,1,0:T(8,128)(2,1)} %param.5) | copy-start | bytes 7077892
  8.0 806.7 %all-gather.8.cloned.1.call-start = ((), (), s32[]{:S(2)}) async-start(), calls=%async_computation.2 | async-start | bytes 128450560 | tf_op jit(solution)/shard_map/all_gather | solution.py:19
  8.8 858.5 %all-gather.12.cloned.1.call-start = ((), (), s32[]{:S(2)}) async-start(), calls=%async_computation.5 | async-start | bytes 2949120 | tf_op jit(solution)/shard_map/all_gather | solution.py:23
  74.6 1019.4 %reduce-scatter.2.cloned.1.call-start = ((), (), s32[]{:S(2)}) async-start(), calls=%async_computation.4 | async-start | bytes 36700160 | tf_op jit(solution)/shard_map/reduce_scatter | solution.py:26
Sparse Core Ops, SparseCore 0:
  8.9 58.7 all-gather.9
  69.3 148.4 all-gather.5
  219.4 595.2 all-gather.7
  816.1 51.1 all-gather.11
  888.2 205.7 reduce-scatter.1
where the time goes:
time: 1100 us
  waiting for transfers between devices  1020 us (93%)
  matrix products  69.8 us (6%)
  between operations  13.8 us (1%)
    all_gather x1, waiting for transfers between devices, per_device(): lax.all_gather(basis_out, 'dp', axis=0, tiled=True)  597 us
    reduce_scatter x1, waiting for transfers between devices, per_device(): lax.psum_scatter(squares.astype(jnp.bfloat16), 'dp', scatter_dimension=1,...  206 us
    all_gather x1, waiting for transfers between devices, per_device(): whole = lax.all_gather(out_grads, 'tensor', axis=2, tiled=True)  143 us
    all_gather x1, waiting for transfers between devices, per_device(): in_cols = lax.all_gather(basis_in, 'dp', axis=0, tiled=True)  58.3 us
    dot_general x1, matrix products, per_device(): jnp.einsum('nsh,hc->nsc', whole, lax.all_gather(basis_out, 'dp', axis=0,...  42.2 us
  transfers between devices with their start and end apart: 5, of which 5 were waited for; matrix products, arithmetic and copies ran while one was open for 4% of the time, Pallas kernels for 0%

commit v1 on v0

v1 whole, which is shorter than its diff:
```python
import jax
import jax.numpy as jnp
from jax import lax
from jax.experimental import pallas as pl
from jax.experimental.pallas import tpu as pltpu
from jax.sharding import PartitionSpec as P

F32 = jnp.float32
BF16 = jnp.bfloat16


def square_kernel(out_ref, in_ref, c_ref):
    total = None
    for n in range(out_ref.shape[0]):
        proj = lax.dot_general(out_ref[n], in_ref[n], (((0,), (0,)), ((), ())), preferred_element_type=F32)
        total = proj * proj if total is None else total + proj * proj
    c_ref[...] = total.astype(c_ref.dtype)


def squares(out_proj, in_proj):
    n, seq, cols = out_proj.shape
    ins = in_proj.shape[2]
    tile = cols
    for t in (512, 256, 128):
        if cols % t == 0:
            tile = t
            break
    return pl.pallas_call(
        square_kernel,
        grid=(cols // tile,),
        in_specs=[
            pl.BlockSpec((n, seq, tile), lambda i: (0, 0, i)),
            pl.BlockSpec((n, seq, ins), lambda i: (0, 0, 0)),
        ],
        out_specs=pl.BlockSpec((tile, ins), lambda i: (i, 0)),
        out_shape=jax.ShapeDtypeStruct((cols, ins), BF16),
        compiler_params=pltpu.CompilerParams(vmem_limit_bytes=48 * 2**20),
        cost_estimate=pl.CostEstimate(
            flops=2 * n * seq * cols * ins, bytes_accessed=2 * (n * seq * (cols + ins) + cols * ins), transcendentals=0
        ),
    )(out_proj, in_proj)


def make(n_dp):
    def swap(x, k):
        return lax.ppermute(x, "dp", [(d, d ^ k) for d in range(n_dp)])

    def per_device(acts, out_grads, basis_in, basis_out, lengths):
        seq = acts.shape[1]
        me = lax.axis_index("dp")
        keep = (jnp.arange(seq, dtype=jnp.int32)[None, :] < lengths[:, None]).astype(acts.dtype)
        kept = (acts * keep[:, :, None])[0]

        def exchange(x, width):
            parts = [lax.dynamic_slice_in_dim(x, (me ^ k) * width, width, axis=1) for k in range(n_dp)]
            return [parts[0]] + [swap(parts[k], k) for k in range(1, n_dp)]

        rows = basis_in.shape[0]
        b0 = basis_in
        b2 = swap(b0, 2)
        b1 = swap(b0, 1)
        b3 = swap(b2, 1)
        blocks = [b0, b1, b2, b3]
        in_local = None
        for k in range(n_dp):
            a = lax.dynamic_slice_in_dim(kept, (me ^ k) * rows, rows, axis=1)
            t = jnp.dot(a, blocks[k], preferred_element_type=F32)
            in_local = t if in_local is None else in_local + t
        in_local = in_local.astype(BF16)

        n_chunks = 3
        step = seq // n_chunks
        wide = out_grads.shape[2] * lax.axis_size("tensor") // n_dp
        outs = []
        in_proj = None
        for j in range(n_chunks):
            g = out_grads[0, j * step : (j + 1) * step]
            whole = lax.all_gather(g, "tensor", axis=1, tiled=True)
            mine = exchange(whole, wide)
            part = [jnp.dot(m, basis_out, preferred_element_type=F32) for m in mine]
            odd = swap(jnp.stack([part[1], part[3]]).astype(BF16), 1)
            s0 = part[0] + odd[0].astype(F32)
            s2 = part[2] + odd[1].astype(F32)
            far = swap(jnp.stack([s2, s0]).astype(BF16), 2)
            even = jnp.stack([(s0 + far[0].astype(F32)).astype(BF16), (s2 + far[1].astype(F32)).astype(BF16)])
            rest = swap(even, 1)
            outs.append(jnp.stack([even[0], rest[0], even[1], rest[1]]))
        in_all = lax.all_gather(in_local, "tensor", axis=1, tiled=True)
        in_proj = jnp.stack(exchange(in_all, in_all.shape[1] // n_dp))
        out_proj = jnp.concatenate(outs, axis=1)
        return squares(out_proj, in_proj)

    return per_device


def solution(mesh):
    in_specs = (
        P(("groups", "dp"), None, None),
        P(("groups", "dp"), None, "tensor"),
        P(("groups", "dp"), "tensor"),
        P(("groups", "dp"), "tensor"),
        P(("groups", "dp")),
    )
    out_specs = P(("groups", "tensor"), "dp")
    return jax.shard_map(
        make(mesh.shape["dp"]), mesh=mesh, in_specs=in_specs, out_specs=out_specs, check_vma=False
    )
```

time: 1100 us -> 445 us (0.40)
  waiting for transfers between devices: 1020 us -> 201 us
  matrix products: 69.8 us -> 150 us
  starting transfers between devices: 0.16 us -> 21.2 us
  Pallas kernels: 0 us -> 19 us
  local copies, waits for them, and re-layouts: 0.01 us -> 18.7 us
  other arithmetic: 0.01 us -> 11.9 us
    all_gather x4, waiting for transfers between devices: 809 us -> 83.9 us  [the longest x3 83.9 us: per_device(): whole = lax.all_gather(g, 'tensor', axis=1, tiled=True)]
    reduce_scatter x1 -> x0, waiting for transfers between devices: 206 us -> none  [per_device(): lax.psum_scatter(squares.astype(jnp.bfloat16), 'dp', scatter_dimension=1,...]
    ppermute x0 -> x24, waiting for transfers between devices: none -> 117 us  [swap(): return lax.ppermute(x, 'dp', [(d, d ^ k) for d in range(n_dp)])]
    dot_general x3 -> x16, matrix products: 69.8 us -> 150 us  [the longest x12 140 us: per_device(): part = [jnp.dot(m, basis_out, preferred_element_type=F32) for m in mine]]
    ppermute x0 -> x24, starting transfers between devices: none -> 21 us  [swap(): return lax.ppermute(x, 'dp', [(d, d ^ k) for d in range(n_dp)])]
    pallas_call x0 -> x1, Pallas kernels: none -> 19 us  [squares(): pl.pallas_call(square_kernel, grid=(cols // tile,), in_specs=[pl.BlockSpe...]
  transfers between devices with their start and end apart: 5 -> 28, of which waited for: 5 -> 9; matrix products, arithmetic and copies ran while one was open for 4% -> 39% of each run, Pallas kernels for 0% -> 0%
where the time goes in v1:
time: 445 us; the launch traced here: 436 us
  waiting for transfers between devices  201 us (45%)
  matrix products  150 us (34%)
  starting transfers between devices  21.2 us (5%)
  Pallas kernels  19 us (4%)
  local copies, waits for them, and re-layouts  18.7 us (4%)
  between operations  14.8 us (3%)
  other arithmetic  11.9 us (3%)
    dot_general x12, matrix products, per_device(): part = [jnp.dot(m, basis_out, preferred_element_type=F32) for m in mine]  140 us
    ppermute x24, waiting for transfers between devices, swap(): return lax.ppermute(x, 'dp', [(d, d ^ k) for d in range(n_dp)])  117 us
    all_gather x3, waiting for transfers between devices, per_device(): whole = lax.all_gather(g, 'tensor', axis=1, tiled=True)  83.9 us
    ppermute x24, starting transfers between devices, swap(): return lax.ppermute(x, 'dp', [(d, d ^ k) for d in range(n_dp)])  21 us
    pallas_call x1, Pallas kernels, squares(): pl.pallas_call(square_kernel, grid=(cols // tile,), in_specs=[pl.BlockSpe...  19 us
    dot_general x4, matrix products, per_device(): t = jnp.dot(a, blocks[k], preferred_element_type=F32)  10 us
  transfers between devices with their start and end apart: 28, of which 9 were waited for; matrix products, arithmetic and copies ran while one was open for 39% of the time, Pallas kernels for 0%

profile of v1, /device:TPU:3, one launch (start us, length us, event | category | flops | bytes accessed | tf_op | source)
XLA Modules:
  0.0 436.3 jit_solution(3007651191650957496)
XLA Ops:
  6.5 3.0 fusion.51
  14.4 42.9 %collective-permute-done.19 = bf16[1024,1024]{1,0:T(8,128)(2,1)} collective-permute-done((bf16[1024,1024]{1,0:T(8,128)(2,1)}, bf16[1024,1024]{1,0:T(8,128)(2,1)}, u32[]{:S(2)}, u32[]{:S(2)}) %collective-permute-start.19) | collective-permute-done | bytes 2097184 | tf_op jit(solution)/shard_map/ppermute | solution.py:46
  58.8 2.4 convolution_add_fusion.5
  61.2 3.4 convolution_add_fusion.4
  64.6 3.3 all-gather.14.cloned.1.call-done
  67.9 2.9 dynamic-slice_bitcast_fusion.2
  72.8 52.4 %all-gather.12.cloned.1.call-done = bf16[1,96,14336]{2,1,0:T(8,128)(2,1)} async-done(((bf16[1,96,3584]{2,1,0:T(8,128)(2,1)}), bf16[1,96,14336]{2,1,0:T(8,128)(2,1)}) %all-gather.12.cloned.1.call-update) | async-done | bytes 2752528 | tf_op jit(solution)/shard_map/all_gather | solution.py:78
  125.2 2.8 dynamic-slice_bitcast_fusion.5
  128.9 14.5 %fusion.25 = f32[96,3584]{1,0:T(8,128)} fusion(bf16[3584,3584]{1,0:T(8,128)(2,1)} %param.8, bf16[1,96,14336]{2,1,0:T(8,128)(2,1)} %all-gather.14.cloned.1.call-done, s32[]{:T(128)S(6)} %select_n.16), kind=kOutput, calls=%fused_computation.70 | convolution fusion | flops 2466250752 | bytes 27754500 | tf_op jit(solution)/shard_map/dot_general | solution.py:80
  143.4 10.9 %fusion.27 = f32[96,3584]{1,0:T(8,128)S(1)} fusion(bf16[3584,3584]{1,0:T(8,128)(2,1)} %param.8, bf16[1,96,14336]{2,1,0:T(8,128)(2,1)} %all-gather.12.cloned.1.call-done, s32[]{:T(128)S(6)} %select_n.16), kind=kOutput, calls=%fused_computation.72 | convolution fusion | flops 2466250752 | bytes 27754500 | tf_op jit(solution)/shard_map/dot_general | solution.py:80
  154.4 28.2 %all-gather.10.cloned.1.call-done = bf16[1,96,14336]{2,1,0:T(8,128)(2,1)} async-done(((bf16[1,96,3584]{2,1,0:T(8,128)(2,1)}), bf16[1,96,14336]{2,1,0:T(8,128)(2,1)}) %all-gather.10.cloned.1.call-update) | async-done | bytes 2752528 | tf_op jit(solution)/shard_map/all_gather | solution.py:78
  182.6 10.8 %fusion.29 = f32[96,3584]{1,0:T(8,128)S(1)} fusion(bf16[3584,3584]{1,0:T(8,128)(2,1)} %param.8, bf16[1,96,14336]{2,1,0:T(8,128)(2,1)} %all-gather.10.cloned.1.call-done, s32[]{:T(128)S(6)} %select_n.16), kind=kOutput, calls=%fused_computation.74 | convolution fusion | flops 2466250752 | bytes 27754500 | tf_op jit(solution)/shard_map/dot_general | solution.py:80
  195.5 3.4 fusion.12
  199.4 13.3 %fusion.5 = bf16[1,96,3584]{2,1,0:T(8,128)(2,1)S(1)} fusion(bf16[96,3584]{1,0:T(8,128)(2,1)} %collective-permute-done.13, bf16[3584,3584]{1,0:T(8,128)(2,1)} %param.8), kind=kOutput, calls=%fused_computation.15 | convolution fusion | flops 2466594816 | bytes 27066368 | tf_op jit(solution)/shard_map/dot_general | solution.py:80
  214.6 10.9 %fusion.4 = bf16[1,96,3584]{2,1,0:T(8,128)(2,1)S(1)} fusion(bf16[96,3584]{1,0:T(8,128)(2,1)S(1)} %collective-permute-done.12, bf16[3584,3584]{1,0:T(8,128)(2,1)} %param.8), kind=kOutput, calls=%fused_computation.14 | convolution fusion | flops 2466594816 | bytes 27066368 | tf_op jit(solution)/shard_map/dot_general | solution.py:80
  225.6 12.9 %fusion.3 = bf16[1,96,3584]{2,1,0:T(8,128)(2,1)S(1)} fusion(bf16[96,3584]{1,0:T(8,128)(2,1)} %collective-permute-done.7, bf16[3584,3584]{1,0:T(8,128)(2,1)} %param.8), kind=kOutput, calls=%fused_computation.13 | convolution fusion | flops 2466594816 | bytes 27066368 | tf_op jit(solution)/shard_map/dot_general | solution.py:80
  238.9 12.7 %fusion.2 = bf16[1,96,3584]{2,1,0:T(8,128)(2,1)S(1)} fusion(bf16[96,3584]{1,0:T(8,128)(2,1)} %collective-permute-done.6, bf16[3584,3584]{1,0:T(8,128)(2,1)} %param.8), kind=kOutput, calls=%fused_computation.12 | convolution fusion | flops 2466594816 | bytes 27066368 | tf_op jit(solution)/shard_map/dot_general | solution.py:80
  252.5 10.6 %fusion.1 = bf16[1,96,3584]{2,1,0:T(8,128)(2,1)S(1)} fusion(bf16[96,3584]{1,0:T(8,128)(2,1)S(1)} %collective-permute-done.1, bf16[3584,3584]{1,0:T(8,128)(2,1)} %param.8), kind=kOutput, calls=%fused_computation.11 | convolution fusion | flops 2466594816 | bytes 27066368 | tf_op jit(solution)/shard_map/dot_general | solution.py:80
  263.4 10.6 %fusion = bf16[1,96,3584]{2,1,0:T(8,128)(2,1)S(1)} fusion(bf16[96,3584]{1,0:T(8,128)(2,1)S(1)} %collective-permute-done, bf16[3584,3584]{1,0:T(8,128)(2,1)} %param.8), kind=kOutput, calls=%fused_computation.10 | convolution fusion | flops 2466594816 | bytes 27066368 | tf_op jit(solution)/shard_map/dot_general | solution.py:80
  275.4 10.9 %convolution_add_fusion = f32[96,3584]{1,0:T(8,128)S(1)} fusion(bf16[96,3584]{1,0:T(8,128)(2,1)} %collective-permute-done.15, bf16[3584,3584]{1,0:T(8,128)(2,1)} %param.8, bf16[2,96,3584]{2,1,0:T(8,128)(2,1)S(1)} %collective-permute-done.14), kind=kOutput, calls=%fused_computation.1 | convolution fusion | flops 2466938880 | bytes 28442624 | tf_op jit(solution)/shard_map/dot_general | solution.py:80
  288.0 10.5 %convolution_add_fusion.1 = f32[96,3584]{1,0:T(8,128)S(1)} fusion(bf16[96,3584]{1,0:T(8,128)(2,1)S(1)} %collective-permute-done.9, bf16[3584,3584]{1,0:T(8,128)(2,1)} %param.8, bf16[2,96,3584]{2,1,0:T(8,128)(2,1)S(1)} %collective-permute-done.8), kind=kOutput, calls=%fused_computation.2 | convolution fusion | flops 2466938880 | bytes 28442624 | tf_op jit(solution)/shard_map/dot_general | solution.py:80
  299.3 10.8 %convolution_add_fusion.2 = f32[96,3584]{1,0:T(8,128)S(1)} fusion(bf16[96,3584]{1,0:T(8,128)(2,1)S(1)} %collective-permute-done.3, bf16[3584,3584]{1,0:T(8,128)(2,1)} %param.8, bf16[2,96,3584]{2,1,0:T(8,128)(2,1)S(1)} %collective-permute-done.2), kind=kOutput, calls=%fused_computation.3 | convolution fusion | flops 2466938880 | bytes 28442624 | tf_op jit(solution)/shard_map/dot_general | solution.py:80
  312.9 5.1 %collective-permute-done.16 = bf16[2,96,3584]{2,1,0:T(8,128)(2,1)S(1)} collective-permute-done((bf16[2,96,3584]{2,1,0:T(8,128)(2,1)S(1)}, bf16[2,96,3584]{2,1,0:T(8,128)(2,1)S(1)}, u32[]{:S(2)}, u32[]{:S(2)}) %collective-permute-start.16) | collective-permute-done | bytes 1376288 | tf_op jit(solution)/shard_map/ppermute | solution.py:46
  319.6 2.3 collective-permute-start.17
  321.9 25.5 %collective-permute-done.10 = bf16[2,96,3584]{2,1,0:T(8,128)(2,1)S(1)} collective-permute-done((bf16[2,96,3584]{2,1,0:T(8,128)(2,1)S(1)}, bf16[2,96,3584]{2,1,0:T(8,128)(2,1)S(1)}, u32[]{:S(2)}, u32[]{:S(2)}) %collective-permute-start.10) | collective-permute-done | bytes 1376288 | tf_op jit(solution)/shard_map/ppermute | solution.py:46
  349.4 2.3 collective-permute-start.11
  355.0 22.0 %collective-permute-done.4 = bf16[2,96,3584]{2,1,0:T(8,128)(2,1)} collective-permute-done((bf16[2,96,3584]{2,1,0:T(8,128)(2,1)}, bf16[2,96,3584]{2,1,0:T(8,128)(2,1)}, u32[]{:S(2)}, u32[]{:S(2)}) %collective-permute-start.4) | collective-permute-done | bytes 1376288 | tf_op jit(solution)/shard_map/ppermute | solution.py:46
  377.0 2.3 collective-permute-start.21
  381.1 10.0 %collective-permute-done.23 = bf16[288,1024]{1,0:T(8,128)(2,1)S(1)} collective-permute-done((bf16[288,1024]{1,0:T(8,128)(2,1)S(1)}, bf16[288,1024]{1,0:T(8,128)(2,1)S(1)}, u32[]{:S(2)}, u32[]{:S(2)}) %collective-permute-start.23) | collective-permute-done | bytes 589856 | tf_op jit(solution)/shard_map/ppermute | solution.py:46
  391.1 11.1 %collective-permute-done.22 = bf16[288,1024]{1,0:T(8,128)(2,1)S(1)} collective-permute-done((bf16[288,1024]{1,0:T(8,128)(2,1)S(1)}, bf16[288,1024]{1,0:T(8,128)(2,1)S(1)}, u32[]{:S(2)}, u32[]{:S(2)}) %collective-permute-start.22) | collective-permute-done | bytes 589856 | tf_op jit(solution)/shard_map/ppermute | solution.py:46
  406.8 3.5 maximum_maximum_fusion.out_ref
  410.4 19.0 %shard_map.55 = bf16[3584,1024]{1,0:T(8,128)(2,1)} custom-call(bf16[4,288,3584]{2,1,0:T(8,128)(2,1)} %maximum_maximum_fusion.out_ref, bf16[4,288,1024]{2,1,0:T(8,128)(2,1)S(1)} %pad_maximum_fusion.in_ref), custom_call_target="tpu_custom_call" | custom-call | flops 8455716864 | bytes 17956864 | tf_op jit(solution)/shard_map/pallas_call | solution.py:28
  (113 shorter events, 34.3 us)
Async XLA Ops:
  6.5 61.4 %all-gather.14.cloned.1.call-start = ((), (), s32[]{:S(2)}) async-start(), calls=%async_computation.3 | async-start | bytes 3440640 | tf_op jit(solution)/shard_map/all_gather | solution.py:78
  9.6 115.7 %all-gather.12.cloned.1.call-start = ((), (), s32[]{:S(2)}) async-start(), calls=%async_computation.2 | async-start | bytes 3440640 | tf_op jit(solution)/shard_map/all_gather | solution.py:78
  10.3 172.2 %all-gather.10.cloned.1.call-start = ((), (), s32[]{:S(2)}) async-start(), calls=%async_computation.1 | async-start | bytes 3440640 | tf_op jit(solution)/shard_map/all_gather | solution.py:78
  10.4 46.9 %collective-permute-start.19 = (bf16[1024,1024]{1,0:T(8,128)(2,1)}, bf16[1024,1024]{1,0:T(8,128)(2,1)}, u32[]{:S(2)}, u32[]{:S(2)}) collective-permute-start(bf16[1024,1024]{1,0:T(8,128)(2,1)} %param.7), channel_id=1, source_target_pairs={{0,2},{1,3},{2,0},{3,1},{4,6},{5,7},{6,4},{7,5},{8,10},{9,11},{10,... | collective-permute-start | bytes 6291464 | tf_op jit(solution)/shard_map/ppermute | solution.py:46
  10.5 48.3 %collective-permute-start.18 = (bf16[1024,1024]{1,0:T(8,128)(2,1)}, bf16[1024,1024]{1,0:T(8,128)(2,1)}, u32[]{:S(2)}, u32[]{:S(2)}) collective-permute-start(bf16[1024,1024]{1,0:T(8,128)(2,1)} %param.7), channel_id=1, source_target_pairs={{0,1},{1,0},{2,3},{3,2},{4,5},{5,4},{6,7},{7,6},{8,9},{9,8},{10,11... | collective-permute-start | bytes 6291464 | tf_op jit(solution)/shard_map/ppermute | solution.py:46
  11.2 340.4 %all-gather.8.cloned.1.call-start = ((), (), s32[]{:S(2)}) async-start(), calls=%async_computation | async-start | bytes 2949120 | tf_op jit(solution)/shard_map/all_gather | solution.py:88
  13.6 47.6 %copy-start.13 = (bf16[1,288,4096]{2,1,0:T(8,128)(2,1)}, bf16[1,288,4096]{2,1,0:T(8,128)(2,1)S(1)}, u32[]{:S(2)}) copy-start(bf16[1,288,4096]{2,1,0:T(8,128)(2,1)S(1)} %broadcast_multiply_fusion) | copy-start | bytes 7077892
  57.3 137.6 %collective-permute-start.20 = (bf16[1024,1024]{1,0:T(8,128)(2,1)}, bf16[1024,1024]{1,0:T(8,128)(2,1)}, u32[]{:S(2)}, u32[]{:S(2)}) collective-permute-start(bf16[1024,1024]{1,0:T(8,128)(2,1)} %collective-permute-done.19), channel_id=1, source_target_pairs={{0,1},{1,0},{2,3},{3,2},{4,5},{5,4},{6,7},{7,6},{8,9},{9,8},{10,11... | collective-permute-start | bytes 6291464 | tf_op jit(solution)/shard_map/ppermute | solution.py:46
  70.8 128.2 %collective-permute-start.13 = (bf16[96,3584]{1,0:T(8,128)(2,1)}, bf16[96,3584]{1,0:T(8,128)(2,1)}, u32[]{:S(2)}, u32[]{:S(2)}) collective-permute-start(bf16[96,3584]{1,0:T(8,128)(2,1)} %get-tuple-element.12), channel_id=1, source_target_pairs={{0,3},{1,2},{2,1},{3,0},{4,7},{5,6},{6,5},{7,4},{8,11},{9,10},{10,... | collective-permute-start | bytes 2064392 | tf_op jit(solution)/shard_map/ppermute | solution.py:46
  71.6 141.0 %collective-permute-start.12 = (bf16[96,3584]{1,0:T(8,128)(2,1)}, bf16[96,3584]{1,0:T(8,128)(2,1)S(1)}, u32[]{:S(2)}, u32[]{:S(2)}) collective-permute-start(bf16[96,3584]{1,0:T(8,128)(2,1)} %get-tuple-element.11), channel_id=1, source_target_pairs={{0,1},{1,0},{2,3},{3,2},{4,5},{5,4},{6,7},{7,6},{8,9},{9,8},{10,11... | collective-permute-start | bytes 2064392 | tf_op jit(solution)/shard_map/ppermute | solution.py:46
  71.6 203.8 %collective-permute-start.15 = (bf16[96,3584]{1,0:T(8,128)(2,1)}, bf16[96,3584]{1,0:T(8,128)(2,1)}, u32[]{:S(2)}, u32[]{:S(2)}) collective-permute-start(bf16[96,3584]{1,0:T(8,128)(2,1)} %get-tuple-element.13), channel_id=1, source_target_pairs={{0,2},{1,3},{2,0},{3,1},{4,6},{5,7},{6,4},{7,5},{8,10},{9,11},{10,... | collective-permute-start | bytes 2064392 | tf_op jit(solution)/shard_map/ppermute | solution.py:46
  128.1 97.4 %collective-permute-start.7 = (bf16[96,3584]{1,0:T(8,128)(2,1)}, bf16[96,3584]{1,0:T(8,128)(2,1)}, u32[]{:S(2)}, u32[]{:S(2)}) collective-permute-start(bf16[96,3584]{1,0:T(8,128)(2,1)} %get-tuple-element.9), channel_id=1, source_target_pairs={{0,3},{1,2},{2,1},{3,0},{4,7},{5,6},{6,5},{7,4},{8,11},{9,10},{10,... | collective-permute-start | bytes 2064392 | tf_op jit(solution)/shard_map/ppermute | solution.py:46
  194.9 43.6 %collective-permute-start.6 = (bf16[96,3584]{1,0:T(8,128)(2,1)}, bf16[96,3584]{1,0:T(8,128)(2,1)}, u32[]{:S(2)}, u32[]{:S(2)}) collective-permute-start(bf16[96,3584]{1,0:T(8,128)(2,1)} %get-tuple-element.8), channel_id=1, source_target_pairs={{0,1},{1,0},{2,3},{3,2},{4,5},{5,4},{6,7},{7,6},{8,9},{9,8},{10,11... | collective-permute-start | bytes 2064392 | tf_op jit(solution)/shard_map/ppermute | solution.py:46
  199.0 13.7 %copy-start.16 = (bf16[96,3584]{1,0:T(8,128)(2,1)S(1)}, bf16[96,3584]{1,0:T(8,128)(2,1)}, u32[]{:S(2)}) copy-start(bf16[96,3584]{1,0:T(8,128)(2,1)} %get-tuple-element.6) | copy-start | bytes 2064388
  199.0 89.0 %collective-permute-start.9 = (bf16[96,3584]{1,0:T(8,128)(2,1)}, bf16[96,3584]{1,0:T(8,128)(2,1)S(1)}, u32[]{:S(2)}, u32[]{:S(2)}) collective-permute-start(bf16[96,3584]{1,0:T(8,128)(2,1)} %get-tuple-element.10), channel_id=1, source_target_pairs={{0,2},{1,3},{2,0},{3,1},{4,6},{5,7},{6,4},{7,5},{8,10},{9,11},{10,... | collective-permute-start | bytes 2064392 | tf_op jit(solution)/shard_map/ppermute | solution.py:46
  212.7 39.0 %collective-permute-start.1 = (bf16[96,3584]{1,0:T(8,128)(2,1)S(1)}, bf16[96,3584]{1,0:T(8,128)(2,1)S(1)}, u32[]{:S(2)}, u32[]{:S(2)}) collective-permute-start(bf16[96,3584]{1,0:T(8,128)(2,1)S(1)} %copy-done.16), channel_id=1, source_target_pairs={{0,3},{1,2},{2,1},{3,0},{4,7},{5,6},{6,5},{7,4},{8,11},{9,10},{10,... | collective-permute-start | bytes 2064392 | tf_op jit(solution)/shard_map/ppermute | solution.py:46
  225.5 37.7 %collective-permute-start = (bf16[96,3584]{1,0:T(8,128)(2,1)S(1)}, bf16[96,3584]{1,0:T(8,128)(2,1)S(1)}, u32[]{:S(2)}, u32[]{:S(2)}) collective-permute-start(bf16[96,3584]{1,0:T(8,128)(2,1)S(1)} %copy-done.15), channel_id=1, source_target_pairs={{0,1},{1,0},{2,3},{3,2},{4,5},{5,4},{6,7},{7,6},{8,9},{9,8},{10,11... | collective-permute-start | bytes 2064392 | tf_op jit(solution)/shard_map/ppermute | solution.py:46
  238.5 60.7 %collective-permute-start.3 = (bf16[96,3584]{1,0:T(8,128)(2,1)S(1)}, bf16[96,3584]{1,0:T(8,128)(2,1)S(1)}, u32[]{:S(2)}, u32[]{:S(2)}) collective-permute-start(bf16[96,3584]{1,0:T(8,128)(2,1)S(1)} %copy-done.14), channel_id=1, source_target_pairs={{0,2},{1,3},{2,0},{3,1},{4,6},{5,7},{6,4},{7,5},{8,10},{9,11},{10,... | collective-permute-start | bytes 2064392 | tf_op jit(solution)/shard_map/ppermute | solution.py:46
  251.7 22.4 %collective-permute-start.14 = (bf16[2,96,3584]{2,1,0:T(8,128)(2,1)S(1)}, bf16[2,96,3584]{2,1,0:T(8,128)(2,1)S(1)}, u32[]{:S(2)}, u32[]{:S(2)}) collective-permute-start(bf16[2,96,3584]{2,1,0:T(8,128)(2,1)S(1)} %pad_maximum_fusion.7), channel_id=1, source_target_pairs={{0,1},{1,0},{2,3},{3,2},{4,5},{5,4},{6,7},{7,6},{8,9},{9,8},{10,11... | collective-permute-start | bytes 4128776 | tf_op jit(solution)/shard_map/ppermute | solution.py:46
  263.3 24.6 %collective-permute-start.8 = (bf16[2,96,3584]{2,1,0:T(8,128)(2,1)S(1)}, bf16[2,96,3584]{2,1,0:T(8,128)(2,1)S(1)}, u32[]{:S(2)}, u32[]{:S(2)}) collective-permute-start(bf16[2,96,3584]{2,1,0:T(8,128)(2,1)S(1)} %pad_maximum_fusion.4), channel_id=1, source_target_pairs={{0,1},{1,0},{2,3},{3,2},{4,5},{5,4},{6,7},{7,6},{8,9},{9,8},{10,11... | collective-permute-start | bytes 4128776 | tf_op jit(solution)/shard_map/ppermute | solution.py:46
  274.1 25.0 %collective-permute-start.2 = (bf16[2,96,3584]{2,1,0:T(8,128)(2,1)S(1)}, bf16[2,96,3584]{2,1,0:T(8,128)(2,1)S(1)}, u32[]{:S(2)}, u32[]{:S(2)}) collective-permute-start(bf16[2,96,3584]{2,1,0:T(8,128)(2,1)S(1)} %pad_maximum_fusion.1), channel_id=1, source_target_pairs={{0,1},{1,0},{2,3},{3,2},{4,5},{5,4},{6,7},{7,6},{8,9},{9,8},{10,11... | collective-permute-start | bytes 4128776 | tf_op jit(solution)/shard_map/ppermute | solution.py:46
  286.6 31.3 %collective-permute-start.16 = (bf16[2,96,3584]{2,1,0:T(8,128)(2,1)S(1)}, bf16[2,96,3584]{2,1,0:T(8,128)(2,1)S(1)}, u32[]{:S(2)}, u32[]{:S(2)}) collective-permute-start(bf16[2,96,3584]{2,1,0:T(8,128)(2,1)S(1)} %pad_maximum_fusion.8), channel_id=1, source_target_pairs={{0,2},{1,3},{2,0},{3,1},{4,6},{5,7},{6,4},{7,5},{8,10},{9,11},{10,... | collective-permute-start | bytes 4128776 | tf_op jit(solution)/shard_map/ppermute | solution.py:46
  298.7 48.7 %collective-permute-start.10 = (bf16[2,96,3584]{2,1,0:T(8,128)(2,1)S(1)}, bf16[2,96,3584]{2,1,0:T(8,128)(2,1)S(1)}, u32[]{:S(2)}, u32[]{:S(2)}) collective-permute-start(bf16[2,96,3584]{2,1,0:T(8,128)(2,1)S(1)} %pad_maximum_fusion.5), channel_id=1, source_target_pairs={{0,2},{1,3},{2,0},{3,1},{4,6},{5,7},{6,4},{7,5},{8,10},{9,11},{10,... | collective-permute-start | bytes 4128776 | tf_op jit(solution)/shard_map/ppermute | solution.py:46
  311.7 65.3 %collective-permute-start.4 = (bf16[2,96,3584]{2,1,0:T(8,128)(2,1)}, bf16[2,96,3584]{2,1,0:T(8,128)(2,1)}, u32[]{:S(2)}, u32[]{:S(2)}) collective-permute-start(bf16[2,96,3584]{2,1,0:T(8,128)(2,1)} %pad_maximum_fusion.2), channel_id=1, source_target_pairs={{0,2},{1,3},{2,0},{3,1},{4,6},{5,7},{6,4},{7,5},{8,10},{9,11},{10,... | collective-permute-start | bytes 4128776 | tf_op jit(solution)/shard_map/ppermute | solution.py:46
  319.6 82.9 %collective-permute-start.17 = (bf16[2,96,3584]{2,1,0:T(8,128)(2,1)}, bf16[2,96,3584]{2,1,0:T(8,128)(2,1)}, u32[]{:S(2)}, u32[]{:S(2)}) collective-permute-start(bf16[2,96,3584]{2,1,0:T(8,128)(2,1)} %pad_maximum_fusion.9), channel_id=1, source_target_pairs={{0,1},{1,0},{2,3},{3,2},{4,5},{5,4},{6,7},{7,6},{8,9},{9,8},{10,11... | collective-permute-start | bytes 4128776 | tf_op jit(solution)/shard_map/ppermute | solution.py:46
  349.4 29.9 %copy-start.2 = (f32[96,3584]{1,0:T(8,128)S(1)}, f32[96,3584]{1,0:T(8,128)}, u32[]{:S(2)}) copy-start(f32[96,3584]{1,0:T(8,128)} %copy-done.1) | copy-start | bytes 4128772
  349.4 54.6 %collective-permute-start.11 = (bf16[2,96,3584]{2,1,0:T(8,128)(2,1)}, bf16[2,96,3584]{2,1,0:T(8,128)(2,1)}, u32[]{:S(2)}, u32[]{:S(2)}) collective-permute-start(bf16[2,96,3584]{2,1,0:T(8,128)(2,1)} %pad_maximum_fusion.6), channel_id=1, source_target_pairs={{0,1},{1,0},{2,3},{3,2},{4,5},{5,4},{6,7},{7,6},{8,9},{9,8},{10,11... | collective-permute-start | bytes 4128776 | tf_op jit(solution)/shard_map/ppermute | solution.py:46
  351.6 27.7 %copy-start.10 = (bf16[2,96,3584]{2,1,0:T(8,128)(2,1)S(1)}, bf16[2,96,3584]{2,1,0:T(8,128)(2,1)}, u32[]{:S(2)}) copy-start(bf16[2,96,3584]{2,1,0:T(8,128)(2,1)} %copy-done.9) | copy-start | bytes 4128772
  353.5 37.6 %collective-permute-start.23 = (bf16[288,1024]{1,0:T(8,128)(2,1)S(1)}, bf16[288,1024]{1,0:T(8,128)(2,1)S(1)}, u32[]{:S(2)}, u32[]{:S(2)}) collective-permute-start(bf16[288,1024]{1,0:T(8,128)(2,1)S(1)} %get-tuple-element.15), channel_id=1, source_target_pairs={{0,3},{1,2},{2,1},{3,0},{4,7},{5,6},{6,5},{7,4},{8,11},{9,10},{10,... | collective-permute-start | bytes 1769480 | tf_op jit(solution)/shard_map/ppermute | solution.py:46
  354.7 47.4 %collective-permute-start.22 = (bf16[288,1024]{1,0:T(8,128)(2,1)S(1)}, bf16[288,1024]{1,0:T(8,128)(2,1)S(1)}, u32[]{:S(2)}, u32[]{:S(2)}) collective-permute-start(bf16[288,1024]{1,0:T(8,128)(2,1)S(1)} %get-tuple-element.16), channel_id=1, source_target_pairs={{0,2},{1,3},{2,0},{3,1},{4,6},{5,7},{6,4},{7,5},{8,10},{9,11},{10,... | collective-permute-start | bytes 1769480 | tf_op jit(solution)/shard_map/ppermute | solution.py:46
  377.0 25.2 %collective-permute-start.21 = (bf16[288,1024]{1,0:T(8,128)(2,1)S(1)}, bf16[288,1024]{1,0:T(8,128)(2,1)S(1)}, u32[]{:S(2)}, u32[]{:S(2)}) collective-permute-start(bf16[288,1024]{1,0:T(8,128)(2,1)S(1)} %get-tuple-element.17), channel_id=1, source_target_pairs={{0,1},{1,0},{2,3},{3,2},{4,5},{5,4},{6,7},{7,6},{8,9},{9,8},{10,11... | collective-permute-start | bytes 1769480 | tf_op jit(solution)/shard_map/ppermute | solution.py:46
  391.1 14.2 %collective-permute-start.5 = (bf16[2,96,3584]{2,1,0:T(8,128)(2,1)S(1)}, bf16[2,96,3584]{2,1,0:T(8,128)(2,1)S(1)}, u32[]{:S(2)}, u32[]{:S(2)}) collective-permute-start(bf16[2,96,3584]{2,1,0:T(8,128)(2,1)S(1)} %pad_maximum_fusion.3), channel_id=1, source_target_pairs={{0,1},{1,0},{2,3},{3,2},{4,5},{5,4},{6,7},{7,6},{8,9},{9,8},{10,11... | collective-permute-start | bytes 4128776 | tf_op jit(solution)/shard_map/ppermute | solution.py:46
  (15 other events, 67.8 us)
Sparse Core Ops, SparseCore 0:
  9.7 58.1 all-gather.13
  69.5 55.7 all-gather.11
  126.8 55.7 all-gather.9
  199.1 49.0 all-gather.7

commit v2 on v0

v2 whole, which is shorter than its diff:
```python
import functools

import jax
import jax.numpy as jnp
from jax import lax
from jax.experimental import pallas as pl
from jax.experimental.pallas import tpu as pltpu
from jax.sharding import PartitionSpec as P

F32 = jnp.float32
BF16 = jnp.bfloat16
ALIGN = 16
CHUNKS = (96, 80, 64, 48)
TILE = 256


def square_kernel(start_ref, out_ref, in_ref, c_ref):
    total = None
    for n in range(in_ref.shape[0]):
        rows = pl.ds(pl.multiple_of(start_ref[n], ALIGN), in_ref.shape[1])
        proj = lax.dot_general(out_ref[rows, :], in_ref[n], (((0,), (0,)), ((), ())), preferred_element_type=F32)
        total = proj * proj if total is None else total + proj * proj
    c_ref[...] = total.astype(c_ref.dtype)


def squares(starts, out_proj, in_proj):
    tokens, cols = out_proj.shape
    n, seq, ins = in_proj.shape
    tile = cols
    for t in (512, 256, 128):
        if cols % t == 0:
            tile = t
            break
    return pl.pallas_call(
        square_kernel,
        grid_spec=pltpu.PrefetchScalarGridSpec(
            num_scalar_prefetch=1,
            grid=(cols // tile,),
            in_specs=[
                pl.BlockSpec((tokens, tile), lambda i, s: (0, i)),
                pl.BlockSpec((n, seq, ins), lambda i, s: (0, 0, 0)),
            ],
            out_specs=pl.BlockSpec((tile, ins), lambda i, s: (i, 0)),
        ),
        out_shape=jax.ShapeDtypeStruct((cols, ins), BF16),
        compiler_params=pltpu.CompilerParams(vmem_limit_bytes=60 * 2**20),
        cost_estimate=pl.CostEstimate(
            flops=2 * n * seq * cols * ins, bytes_accessed=2 * (n * seq * (cols + ins) + cols * ins), transcendentals=0
        ),
    )(starts, out_proj, in_proj)


def product_kernel(*refs):
    x_refs, basis_ref, given_ref, held_ref, rows_ref = refs[:4], refs[4], refs[5], refs[6], refs[7]
    r = x_refs[0].shape[0]

    @pl.when(pl.program_id(0) == 0)
    def _():
        for at, k in enumerate((1, 3, 0, 2)):
            rows_ref[at * r : (at + 1) * r, :] = x_refs[k][...]

    total = jnp.dot(rows_ref[...], basis_ref[...], preferred_element_type=F32)
    given_ref[...] = total[: 2 * r].astype(given_ref.dtype)
    held_ref[...] = total[2 * r :]


def products(blocks, basis):
    r, depth = blocks[0].shape
    cols = basis.shape[1]
    return pl.pallas_call(
        product_kernel,
        grid=(cols // TILE,),
        in_specs=[pl.BlockSpec((r, depth), lambda i: (0, 0))] * 4 + [pl.BlockSpec((depth, TILE), lambda i: (0, i))],
        out_specs=[pl.BlockSpec((2 * r, TILE), lambda i: (0, i))] * 2,
        out_shape=[jax.ShapeDtypeStruct((2 * r, cols), BF16), jax.ShapeDtypeStruct((2 * r, cols), F32)],
        scratch_shapes=[pltpu.VMEM((4 * r, depth), BF16)],
        compiler_params=pltpu.CompilerParams(vmem_limit_bytes=32 * 2**20),
        cost_estimate=pl.CostEstimate(flops=1, bytes_accessed=1, transcendentals=0),
    )(*blocks, basis)


def pieces_kernel(n_chunks, *refs):
    own, rest, in_ref, out_ref, rows_ref = refs[:n_chunks], refs[n_chunks : 2 * n_chunks], refs[-3], refs[-2], refs[-1]
    total = None
    for k in range(4):
        at = 0
        for part in own if k % 2 == 0 else rest:
            r = part.shape[0] // 2
            rows_ref[k, at : at + r, :] = part[(k // 2) * r : (k // 2 + 1) * r, :]
            at += r
        proj = lax.dot_general(rows_ref[k], in_ref[k], (((0,), (0,)), ((), ())), preferred_element_type=F32)
        total = proj * proj if total is None else total + proj * proj
    out_ref[...] = total.astype(out_ref.dtype)


def squares_of_pieces(own, rest, in_proj):
    cols = own[0].shape[1]
    n, seq, ins = in_proj.shape
    return pl.pallas_call(
        functools.partial(pieces_kernel, len(own)),
        grid=(cols // TILE,),
        in_specs=[pl.BlockSpec((p.shape[0], TILE), lambda i: (0, i)) for p in own + rest]
        + [pl.BlockSpec((n, seq, ins), lambda i: (0, 0, 0))],
        out_specs=pl.BlockSpec((TILE, ins), lambda i: (i, 0)),
        out_shape=jax.ShapeDtypeStruct((cols, ins), BF16),
        scratch_shapes=[pltpu.VMEM((n, seq, TILE), BF16)],
        compiler_params=pltpu.CompilerParams(vmem_limit_bytes=60 * 2**20),
        cost_estimate=pl.CostEstimate(flops=1, bytes_accessed=1, transcendentals=0),
    )(*own, *rest, in_proj)


def swap_dp(x, k, n_dp):
    return lax.ppermute(x, "dp", [(d, d ^ k) for d in range(n_dp)])


def project_in(kept, blocks, me):
    rows = blocks[0].shape[0]
    total = None
    for k, b in enumerate(blocks):
        a = lax.dynamic_slice_in_dim(kept, (me ^ k) * rows, rows, axis=1)
        t = jnp.dot(a, b, preferred_element_type=F32)
        total = t if total is None else total + t
    return total.astype(BF16)


def mask_acts(acts, lengths):
    keep = (jnp.arange(acts.shape[1], dtype=jnp.int32)[None, :] < lengths[:, None]).astype(acts.dtype)
    return (acts * keep[:, :, None])[0]


def general(n_dp, acts, out_grads, basis_in, basis_out, lengths):
    seq = acts.shape[1]
    me = lax.axis_index("dp")
    kept = mask_acts(acts, lengths)

    def exchange(x, width):
        parts = [lax.dynamic_slice_in_dim(x, (me ^ k) * width, width, axis=1) for k in range(n_dp)]
        return [parts[0]] + [swap_dp(parts[k], k, n_dp) for k in range(1, n_dp)]

    far = swap_dp(basis_in, 2, n_dp)
    blocks = [basis_in, swap_dp(basis_in, 1, n_dp), far, swap_dp(far, 1, n_dp)]
    in_local = project_in(kept, blocks, me)
    n_chunks = 3
    step = seq // n_chunks
    outs = []
    for j in range(n_chunks):
        g = out_grads[0, j * step : (j + 1) * step]
        whole = lax.all_gather(g, "tensor", axis=1, tiled=True)
        mine = jnp.concatenate(exchange(whole, whole.shape[1] // n_dp), axis=0)
        part = jnp.dot(mine, basis_out, preferred_element_type=F32)
        part = part.reshape(n_dp, step, -1)
        odd = swap_dp(part[1::2].astype(BF16), 1, n_dp)
        s0 = part[0] + odd[0].astype(F32)
        s2 = part[2] + odd[1].astype(F32)
        far = swap_dp(jnp.stack([s2, s0]).astype(BF16), 2, n_dp)
        even = jnp.stack([s0 + far[0].astype(F32), s2 + far[1].astype(F32)]).astype(BF16)
        rest = swap_dp(even, 1, n_dp)
        outs.append(jnp.stack([even[0], rest[0], even[1], rest[1]]))
    in_all = lax.all_gather(in_local, "tensor", axis=1, tiled=True)
    in_proj = jnp.stack(exchange(in_all, in_all.shape[1] // n_dp))
    out_proj = jnp.concatenate(outs, axis=1).reshape(n_dp * seq, -1)
    return squares(jnp.arange(n_dp, dtype=jnp.int32) * seq, out_proj, in_proj)


def tie(v, *after):
    return lax.optimization_barrier((v,) + after)[0]


def special(acts, out_grads, basis_in, basis_out, lengths):
    me = lax.axis_index("dp")
    z = lax.axis_index("tensor")
    swap = lambda v, k: swap_dp(v, k, 4)
    shift = lambda v, k: lax.ppermute(v, "tensor", [(i, (i + k) % 4) for i in range(4)])

    far = swap(basis_in, 2)
    blocks = [basis_in, swap(basis_in, 1), far, swap(far, 1)]
    in_local = project_in(mask_acts(acts, lengths), blocks, me)

    wholes = []
    at = 0
    for r in CHUNKS:
        wholes.append(lax.all_gather(out_grads[0, at : at + r], "tensor", axis=0))
        at += r

    def parts_of(whole):
        return [lax.dynamic_index_in_dim(whole, me ^ k, 0, keepdims=False) for k in range(4)]

    def spread(parts):
        return [parts[0]] + [swap(parts[k], k) for k in range(1, 4)]

    n = len(CHUNKS)
    own, rest = [], []
    parts = [None] * n
    parts[0] = parts_of(tie(wholes[0], far))
    mine = spread(parts[0])
    after = [in_local]
    for i, r in enumerate(CHUNKS):
        if i >= 1 and i + 1 < n:
            parts[i + 1] = parts_of(wholes[i + 1])
            after += parts[i + 1]
        mine[0] = tie(mine[0], *after)
        given, held = products(mine, basis_out)
        sums = held + swap(given, 1).astype(F32)
        far = swap(sums.astype(BF16), 2)
        after = [far]
        if i == 0:
            parts[1] = parts_of(tie(wholes[1], in_local))
            got = [in_local] + [shift(in_local, k) for k in (1, 2, 3)]
            after += got
        if i == 1:
            in_parts = []
            for k in range(4):
                by = (z - (me ^ k)) % 4
                in_parts.append(lax.select_n(by, *got))
            in_all = [in_parts[0]] + [swap(in_parts[k], k) for k in range(1, 4)]
            after += in_all
        if i + 1 < n:
            mine = spread(parts[i + 1])
        full = jnp.concatenate([sums[:r] + far[r:].astype(F32), sums[r:] + far[:r].astype(F32)]).astype(BF16)
        own.append(full)
        rest.append(swap(full, 1))
    in_all = jnp.stack(in_all)
    return squares_of_pieces(own, rest, in_all)


def per_device(sizes, acts, out_grads, basis_in, basis_out, lengths):
    if sizes == (4, 4) and sum(CHUNKS) == acts.shape[1]:
        return special(acts, out_grads, basis_in, basis_out, lengths)
    return general(sizes[1], acts, out_grads, basis_in, basis_out, lengths)


def solution(mesh):
    in_specs = (
        P(("groups", "dp"), None, None),
        P(("groups", "dp"), None, "tensor"),
        P(("groups", "dp"), "tensor"),
        P(("groups", "dp"), "tensor"),
        P(("groups", "dp")),
    )
    out_specs = P(("groups", "tensor"), "dp")
    sizes = (mesh.shape["tensor"], mesh.shape["dp"])
    return jax.shard_map(
        functools.partial(per_device, sizes), mesh=mesh, in_specs=in_specs, out_specs=out_specs, check_vma=False
    )
```

time: 1100 us -> 443 us (0.40)
  waiting for transfers between devices: 1020 us -> 247 us
  Pallas kernels: 0 us -> 91.3 us
  matrix products: 69.8 us -> 9 us
  local copies, waits for them, and re-layouts: 0.01 us -> 30.8 us
  starting transfers between devices: 0.16 us -> 30.5 us
  other arithmetic: 0.01 us -> 15.8 us
    all_gather x4, waiting for transfers between devices: 809 us -> 24.6 us  [special(): wholes.append(lax.all_gather(out_grads[0, at:at + r], 'tensor', axis=0))]
    ppermute x0 -> x33, waiting for transfers between devices: none -> 222 us  [the longest x30 174 us: swap_dp(): return lax.ppermute(x, 'dp', [(d, d ^ k) for d in range(n_dp)])]
    reduce_scatter x1 -> x0, waiting for transfers between devices: 206 us -> none  [per_device(): lax.psum_scatter(squares.astype(jnp.bfloat16), 'dp', scatter_dimension=1,...]
    pallas_call x0 -> x5, Pallas kernels: none -> 91.3 us  [the longest x4 69.8 us: products(): pl.pallas_call(product_kernel, grid=(cols // TILE,), in_specs=[pl.BlockSp...]
    dot_general x3 -> x4, matrix products: 69.8 us -> 9 us  [project_in(): t = jnp.dot(a, b, preferred_element_type=F32)]
    ppermute x0 -> x33, starting transfers between devices: none -> 30.3 us  [the longest x30 28.2 us: swap_dp(): return lax.ppermute(x, 'dp', [(d, d ^ k) for d in range(n_dp)])]
    unnamed x2 -> x62, local copies, waits for them, and re-layouts: 0.01 us -> 14.4 us
  transfers between devices with their start and end apart: 5 -> 37, of which waited for: 5 -> 17; matrix products, arithmetic and copies ran while one was open for 4% -> 9% of each run, Pallas kernels for 0% -> 8%
where the time goes in v2:
time: 443 us; the launch traced here: 439 us
  waiting for transfers between devices  247 us (56%)
  Pallas kernels  91.3 us (21%)
  local copies, waits for them, and re-layouts  30.8 us (7%)
  starting transfers between devices  30.5 us (7%)
  other arithmetic  15.8 us (4%)
  between operations  14.2 us (3%)
  matrix products  9 us (2%)
    ppermute x30, waiting for transfers between devices, swap_dp(): return lax.ppermute(x, 'dp', [(d, d ^ k) for d in range(n_dp)])  174 us
    pallas_call x4, Pallas kernels, products(): pl.pallas_call(product_kernel, grid=(cols // TILE,), in_specs=[pl.BlockSp...  69.8 us
    ppermute x3, waiting for transfers between devices, special(): lax.ppermute(v, 'tensor', [(i, (i + k) % 4) for i in range(4)])  48.4 us
    ppermute x30, starting transfers between devices, swap_dp(): return lax.ppermute(x, 'dp', [(d, d ^ k) for d in range(n_dp)])  28.2 us
    all_gather x4, waiting for transfers between devices, special(): wholes.append(lax.all_gather(out_grads[0, at:at + r], 'tensor', axis=0))  24.6 us
    pallas_call x1, Pallas kernels, squares_of_pieces(): pl.pallas_call(functools.partial(pieces_kernel, len(own)), grid=(cols //...  21.6 us
    unnamed x62, local copies, waits for them, and re-layouts  14.4 us
    dot_general x4, matrix products, project_in(): t = jnp.dot(a, b, preferred_element_type=F32)  9 us
  transfers between devices with their start and end apart: 37, of which 17 were waited for; matrix products, arithmetic and copies ran while one was open for 9% of the time, Pallas kernels for 8%

profile of v2, /device:TPU:3, one launch (start us, length us, event | category | flops | bytes accessed | tf_op | source)
XLA Modules:
  0.0 438.6 jit_solution(849402080800927241)
XLA Ops:
  6.5 2.2 slice.60
  9.6 1.9 slice.65
  12.3 43.4 %collective-permute-done = bf16[1024,1024]{1,0:T(8,128)(2,1)} collective-permute-done((bf16[1024,1024]{1,0:T(8,128)(2,1)}, bf16[1024,1024]{1,0:T(8,128)(2,1)}, u32[]{:S(2)}, u32[]{:S(2)}) %collective-permute-start) | collective-permute-done | bytes 2097184 | tf_op jit(solution)/shard_map/ppermute | solution.py:113
  59.7 7.4 %all-gather.5.cloned.1.call-done = bf16[4,96,3584]{2,1,0:T(8,128)(2,1)} async-done(((bf16[1,96,3584]{2,1,0:T(8,128)(2,1)}), bf16[4,96,3584]{2,1,0:T(8,128)(2,1)}) %all-gather.5.cloned.1.call-update) | async-done | bytes 2752528 | tf_op jit(solution)/shard_map/all_gather | solution.py:182
  67.1 1.9 dynamic-slice_bitcast_fusion
  71.5 2.4 convolution_add_fusion.2
  73.9 2.5 convolution_add_fusion.1
  76.4 3.3 fusion.2
  79.8 7.2 %collective-permute-done.4.refs_2_ = bf16[96,3584]{1,0:T(8,128)(2,1)S(1)} collective-permute-done((bf16[96,3584]{1,0:T(8,128)(2,1)S(1)}, bf16[96,3584]{1,0:T(8,128)(2,1)S(1)}, u32[]{:S(2)}, u32[]{:S(2)}) %collective-permute-start.4) | collective-permute-done | bytes 688160 | tf_op jit(solution)/shard_map/ppermute | solution.py:113
  86.9 15.2 %collective-permute-done.5.refs_3_ = bf16[96,3584]{1,0:T(8,128)(2,1)S(1)} collective-permute-done((bf16[96,3584]{1,0:T(8,128)(2,1)S(1)}, bf16[96,3584]{1,0:T(8,128)(2,1)S(1)}, u32[]{:S(2)}, u32[]{:S(2)}) %collective-permute-start.5) | collective-permute-done | bytes 688160 | tf_op jit(solution)/shard_map/ppermute | solution.py:113
  102.1 19.1 %shard_map.55 = (bf16[192,3584]{1,0:T(8,128)(2,1)}, f32[192,3584]{1,0:T(8,128)S(1)}) custom-call(bf16[96,3584]{1,0:T(8,128)(2,1)S(1)} %get-tuple-element.20.refs_0_, bf16[96,3584]{1,0:T(8,128)(2,1)S(1)} %collective-permute-done.3.refs_1_, bf16[96,3584]{1,0:T(8,128)(2,1)S(1)} %collective-permute-done.4.refs_2_, ...), custom_call_target="tpu_custom_call" | custom-call | flops 1 | bytes 1 | tf_op jit(solution)/shard_map/pallas_call | solution.py:70
  121.2 1.8 slice.66
  124.7 3.8 fusion.26
  130.9 2.8 dynamic-slice_bitcast_fusion.4
  135.0 44.1 %collective-permute-done.10 = bf16[288,1024]{1,0:T(8,128)(2,1)S(1)} collective-permute-done((bf16[288,1024]{1,0:T(8,128)(2,1)}, bf16[288,1024]{1,0:T(8,128)(2,1)S(1)}, u32[]{:S(2)}, u32[]{:S(2)}) %collective-permute-start.10) | collective-permute-done | bytes 589856 | tf_op jit(solution)/shard_map/ppermute | solution.py:173
  179.9 4.3 collective-permute-start.12
  186.4 17.2 %all-gather.9.cloned.1.call-done = bf16[4,64,3584]{2,1,0:T(8,128)(2,1)} async-done(((bf16[1,64,3584]{2,1,0:T(8,128)(2,1)}), bf16[4,64,3584]{2,1,0:T(8,128)(2,1)}) %all-gather.9.cloned.1.call-update) | async-done | bytes 1835024 | tf_op jit(solution)/shard_map/all_gather | solution.py:182
  203.5 2.6 dynamic-slice_bitcast_fusion.8
  206.1 4.4 collective-permute-done.9
  216.2 18.2 %shard_map.56 = (bf16[160,3584]{1,0:T(8,128)(2,1)}, f32[160,3584]{1,0:T(8,128)S(1)}) custom-call(bf16[80,3584]{1,0:T(8,128)(2,1)S(1)} %get-tuple-element.24.refs_0_, bf16[80,3584]{1,0:T(8,128)(2,1)S(1)} %copy-done.1, bf16[80,3584]{1,0:T(8,128)(2,1)S(1)} %copy-done.3, bf16[80,3584]{1,0:T(8,128)(2,1)S(1)} %copy-done.5, bf16[3584,3584]{1,0:T(8,128)(2,1)} %refs_4_.7), custom_call_target="tpu_custom_call" | custom-call | flops 1 | bytes 1 | tf_op jit(solution)/shard_map/pallas_call | solution.py:70
  238.2 3.6 fusion.25
  243.2 2.4 select_select_fusion
  248.9 32.2 %collective-permute-done.17 = bf16[288,1024]{1,0:T(8,128)(2,1)S(1)} collective-permute-done((bf16[288,1024]{1,0:T(8,128)(2,1)S(1)}, bf16[288,1024]{1,0:T(8,128)(2,1)S(1)}, u32[]{:S(2)}, u32[]{:S(2)}) %collective-permute-start.17) | collective-permute-done | bytes 589856 | tf_op jit(solution)/shard_map/ppermute | solution.py:113
  281.9 3.3 collective-permute-start.21
  286.6 8.5 %collective-permute-done.18 = bf16[288,1024]{1,0:T(8,128)(2,1)S(1)} collective-permute-done((bf16[288,1024]{1,0:T(8,128)(2,1)}, bf16[288,1024]{1,0:T(8,128)(2,1)S(1)}, u32[]{:S(2)}, u32[]{:S(2)}) %collective-permute-start.18) | collective-permute-done | bytes 589856 | tf_op jit(solution)/shard_map/ppermute | solution.py:113
  295.0 8.5 %collective-permute-done.20.refs_2_ = bf16[64,3584]{1,0:T(8,128)(2,1)S(1)} collective-permute-done((bf16[64,3584]{1,0:T(8,128)(2,1)}, bf16[64,3584]{1,0:T(8,128)(2,1)S(1)}, u32[]{:S(2)}, u32[]{:S(2)}) %collective-permute-start.20) | collective-permute-done | bytes 458784 | tf_op jit(solution)/shard_map/ppermute | solution.py:113
  303.5 10.3 %collective-permute-done.21.refs_3_ = bf16[64,3584]{1,0:T(8,128)(2,1)S(1)} collective-permute-done((bf16[64,3584]{1,0:T(8,128)(2,1)S(1)}, bf16[64,3584]{1,0:T(8,128)(2,1)S(1)}, u32[]{:S(2)}, u32[]{:S(2)}) %collective-permute-start.21) | collective-permute-done | bytes 458784 | tf_op jit(solution)/shard_map/ppermute | solution.py:113
  313.9 16.7 %shard_map.57 = (bf16[128,3584]{1,0:T(8,128)(2,1)S(1)}, f32[128,3584]{1,0:T(8,128)S(1)}) custom-call(bf16[64,3584]{1,0:T(8,128)(2,1)S(1)} %get-tuple-element.27.refs_0_, bf16[64,3584]{1,0:T(8,128)(2,1)S(1)} %collective-permute-done.19.refs_1_, bf16[64,3584]{1,0:T(8,128)(2,1)S(1)} %collective-permute-done.20.refs_2_, ...), custom_call_target="tpu_custom_call" | custom-call | flops 1 | bytes 1 | tf_op jit(solution)/shard_map/pallas_call | solution.py:70
  337.2 30.7 %collective-permute-done.23 = bf16[128,3584]{1,0:T(8,128)(2,1)S(1)} collective-permute-done((bf16[128,3584]{1,0:T(8,128)(2,1)S(1)}, bf16[128,3584]{1,0:T(8,128)(2,1)S(1)}, u32[]{:S(2)}, u32[]{:S(2)}) %collective-permute-start.23) | collective-permute-done | bytes 917536 | tf_op jit(solution)/shard_map/ppermute | solution.py:113
  367.9 15.8 %shard_map.58 = (bf16[96,3584]{1,0:T(8,128)(2,1)S(1)}, f32[96,3584]{1,0:T(8,128)S(1)}) custom-call(bf16[48,3584]{1,0:T(8,128)(2,1)S(1)} %get-tuple-element.30.refs_0_, bf16[48,3584]{1,0:T(8,128)(2,1)S(1)} %collective-permute-done.24.refs_1_, bf16[48,3584]{1,0:T(8,128)(2,1)S(1)} %collective-permute-done.25.refs_2_, ...), custom_call_target="tpu_custom_call" | custom-call | flops 1 | bytes 1 | tf_op jit(solution)/shard_map/pallas_call | solution.py:70
  389.2 15.0 %collective-permute-done.28 = bf16[96,3584]{1,0:T(8,128)(2,1)S(1)} collective-permute-done((bf16[96,3584]{1,0:T(8,128)(2,1)S(1)}, bf16[96,3584]{1,0:T(8,128)(2,1)S(1)}, u32[]{:S(2)}, u32[]{:S(2)}) %collective-permute-start.28) | collective-permute-done | bytes 688160 | tf_op jit(solution)/shard_map/ppermute | solution.py:113
  410.5 21.6 %shard_map.59 = bf16[3584,1024]{1,0:T(8,128)(2,1)} custom-call(bf16[192,3584]{1,0:T(8,128)(2,1)} %copy-done.8, bf16[160,3584]{1,0:T(8,128)(2,1)} %copy-done.9, bf16[128,3584]{1,0:T(8,128)(2,1)} %copy-done.10, bf16[96,3584]{1,0:T(8,128)(2,1)} %copy-done.11, bf16[192,3584]{1,0:T(8,128)(2,1)} %copy-done.15, bf16[160,3584]{1,0:T(8,128)(2,1)} %copy-done.16, ...), custom_call_target="tpu_custom_call" | custom-call | flops 1 | bytes 1 | tf_op jit(solution)/shard_map/pallas_call | solution.py:99
  (141 shorter events, 50.1 us)
Async XLA Ops:
  6.5 60.6 %all-gather.5.cloned.1.call-start = ((), (), s32[]{:S(2)}) async-start(), calls=%async_computation | async-start | bytes 3440640 | tf_op jit(solution)/shard_map/all_gather | solution.py:182
  8.8 122.2 %all-gather.7.cloned.1.call-start = ((), (), s32[]{:S(2)}) async-start(), calls=%async_computation.1 | async-start | bytes 2867200 | tf_op jit(solution)/shard_map/all_gather | solution.py:182
  8.8 46.9 %collective-permute-start = (bf16[1024,1024]{1,0:T(8,128)(2,1)}, bf16[1024,1024]{1,0:T(8,128)(2,1)}, u32[]{:S(2)}, u32[]{:S(2)}) collective-permute-start(bf16[1024,1024]{1,0:T(8,128)(2,1)} %param.7), channel_id=1, source_target_pairs={{0,2},{1,3},{2,0},{3,1},{4,6},{5,7},{6,4},{7,5},{8,10},{9,11},{10,... | collective-permute-start | bytes 6291464 | tf_op jit(solution)/shard_map/ppermute | solution.py:113
  8.9 62.6 %collective-permute-start.1 = (bf16[1024,1024]{1,0:T(8,128)(2,1)}, bf16[1024,1024]{1,0:T(8,128)(2,1)}, u32[]{:S(2)}, u32[]{:S(2)}) collective-permute-start(bf16[1024,1024]{1,0:T(8,128)(2,1)} %param.7), channel_id=1, source_target_pairs={{0,1},{1,0},{2,3},{3,2},{4,5},{5,4},{6,7},{7,6},{8,9},{9,8},{10,11... | collective-permute-start | bytes 6291464 | tf_op jit(solution)/shard_map/ppermute | solution.py:113
  11.6 192.0 %all-gather.9.cloned.1.call-start = ((), (), s32[]{:S(2)}) async-start(), calls=%async_computation.2 | async-start | bytes 2293760 | tf_op jit(solution)/shard_map/all_gather | solution.py:182
  55.7 20.7 %collective-permute-start.2 = (bf16[1024,1024]{1,0:T(8,128)(2,1)}, bf16[1024,1024]{1,0:T(8,128)(2,1)}, u32[]{:S(2)}, u32[]{:S(2)}) collective-permute-start(bf16[1024,1024]{1,0:T(8,128)(2,1)} %collective-permute-done), channel_id=1, source_target_pairs={{0,1},{1,0},{2,3},{3,2},{4,5},{5,4},{6,7},{7,6},{8,9},{9,8},{10,11... | collective-permute-start | bytes 6291464 | tf_op jit(solution)/shard_map/ppermute | solution.py:113
  69.0 10.7 %collective-permute-start.3 = (bf16[96,3584]{1,0:T(8,128)(2,1)S(1)}, bf16[96,3584]{1,0:T(8,128)(2,1)S(1)}, u32[]{:S(2)}, u32[]{:S(2)}) collective-permute-start(bf16[96,3584]{1,0:T(8,128)(2,1)S(1)} %get-tuple-element.49), channel_id=1, source_target_pairs={{0,1},{1,0},{2,3},{3,2},{4,5},{5,4},{6,7},{7,6},{8,9},{9,8},{10,11... | collective-permute-start | bytes 2064392 | tf_op jit(solution)/shard_map/ppermute | solution.py:113
  69.8 17.1 %collective-permute-start.4 = (bf16[96,3584]{1,0:T(8,128)(2,1)S(1)}, bf16[96,3584]{1,0:T(8,128)(2,1)S(1)}, u32[]{:S(2)}, u32[]{:S(2)}) collective-permute-start(bf16[96,3584]{1,0:T(8,128)(2,1)S(1)} %get-tuple-element.48), channel_id=1, source_target_pairs={{0,2},{1,3},{2,0},{3,1},{4,6},{5,7},{6,4},{7,5},{8,10},{9,11},{10,... | collective-permute-start | bytes 2064392 | tf_op jit(solution)/shard_map/ppermute | solution.py:113
  70.1 32.0 %collective-permute-start.5 = (bf16[96,3584]{1,0:T(8,128)(2,1)S(1)}, bf16[96,3584]{1,0:T(8,128)(2,1)S(1)}, u32[]{:S(2)}, u32[]{:S(2)}) collective-permute-start(bf16[96,3584]{1,0:T(8,128)(2,1)S(1)} %get-tuple-element.47), channel_id=1, source_target_pairs={{0,3},{1,2},{2,1},{3,0},{4,7},{5,6},{6,5},{7,4},{8,11},{9,10},{10,... | collective-permute-start | bytes 2064392 | tf_op jit(solution)/shard_map/ppermute | solution.py:113
  123.1 162.1 %all-gather.11.cloned.1.call-start = ((), (), s32[]{:S(2)}) async-start(), calls=%async_computation.3 | async-start | bytes 1720320 | tf_op jit(solution)/shard_map/all_gather | solution.py:182
  128.5 82.0 %collective-permute-start.7 = (bf16[192,3584]{1,0:T(8,128)(2,1)}, bf16[192,3584]{1,0:T(8,128)(2,1)}, u32[]{:S(2)}, u32[]{:S(2)}) collective-permute-start(bf16[192,3584]{1,0:T(8,128)(2,1)} %get-tuple-element.39), channel_id=1, source_target_pairs={{0,2},{1,3},{2,0},{3,1},{4,6},{5,7},{6,4},{7,5},{8,10},{9,11},{10,... | collective-permute-start | bytes 4128776 | tf_op jit(solution)/shard_map/ppermute | solution.py:113
  128.8 50.3 %collective-permute-start.10 = (bf16[288,1024]{1,0:T(8,128)(2,1)}, bf16[288,1024]{1,0:T(8,128)(2,1)S(1)}, u32[]{:S(2)}, u32[]{:S(2)}) collective-permute-start(bf16[288,1024]{1,0:T(8,128)(2,1)} %fusion.2), channel_id=1, source_target_pairs={{0,12},{4,0},{8,4},{12,8},{1,13},{5,1},{9,5},{13,9},{2,14},{6,2},{... | collective-permute-start | bytes 1769480 | tf_op jit(solution)/shard_map/ppermute | solution.py:173
  129.3 54.9 %collective-permute-start.8 = (bf16[288,1024]{1,0:T(8,128)(2,1)}, bf16[288,1024]{1,0:T(8,128)(2,1)S(1)}, u32[]{:S(2)}, u32[]{:S(2)}) collective-permute-start(bf16[288,1024]{1,0:T(8,128)(2,1)} %fusion.2), channel_id=1, source_target_pairs={{0,4},{4,8},{8,12},{12,0},{1,5},{5,9},{9,13},{13,1},{2,6},{6,10},{... | collective-permute-start | bytes 1769480 | tf_op jit(solution)/shard_map/ppermute | solution.py:173
  130.3 80.2 %collective-permute-start.9 = (bf16[288,1024]{1,0:T(8,128)(2,1)}, bf16[288,1024]{1,0:T(8,128)(2,1)}, u32[]{:S(2)}, u32[]{:S(2)}) collective-permute-start(bf16[288,1024]{1,0:T(8,128)(2,1)} %fusion.2), channel_id=1, source_target_pairs={{0,8},{4,12},{8,0},{12,4},{1,9},{5,13},{9,1},{13,5},{2,10},{6,14},... | collective-permute-start | bytes 1769480 | tf_op jit(solution)/shard_map/ppermute | solution.py:173
  133.8 76.8 %collective-permute-start.11 = (bf16[80,3584]{1,0:T(8,128)(2,1)}, bf16[80,3584]{1,0:T(8,128)(2,1)S(1)}, u32[]{:S(2)}, u32[]{:S(2)}) collective-permute-start(bf16[80,3584]{1,0:T(8,128)(2,1)} %get-tuple-element.57), channel_id=1, source_target_pairs={{0,1},{1,0},{2,3},{3,2},{4,5},{5,4},{6,7},{7,6},{8,9},{9,8},{10,11... | collective-permute-start | bytes 1720328 | tf_op jit(solution)/shard_map/ppermute | solution.py:113
  179.9 31.5 %collective-permute-start.12 = (bf16[80,3584]{1,0:T(8,128)(2,1)}, bf16[80,3584]{1,0:T(8,128)(2,1)S(1)}, u32[]{:S(2)}, u32[]{:S(2)}) collective-permute-start(bf16[80,3584]{1,0:T(8,128)(2,1)} %get-tuple-element.56), channel_id=1, source_target_pairs={{0,2},{1,3},{2,0},{3,1},{4,6},{5,7},{6,4},{7,5},{8,10},{9,11},{10,... | collective-permute-start | bytes 1720328 | tf_op jit(solution)/shard_map/ppermute | solution.py:113
  185.1 27.2 %collective-permute-start.13 = (bf16[80,3584]{1,0:T(8,128)(2,1)}, bf16[80,3584]{1,0:T(8,128)(2,1)S(1)}, u32[]{:S(2)}, u32[]{:S(2)}) collective-permute-start(bf16[80,3584]{1,0:T(8,128)(2,1)} %get-tuple-element.55), channel_id=1, source_target_pairs={{0,3},{1,2},{2,1},{3,0},{4,7},{5,6},{6,5},{7,4},{8,11},{9,10},{10,... | collective-permute-start | bytes 1720328 | tf_op jit(solution)/shard_map/ppermute | solution.py:113
  241.7 53.3 %collective-permute-start.15 = (bf16[160,3584]{1,0:T(8,128)(2,1)}, bf16[160,3584]{1,0:T(8,128)(2,1)}, u32[]{:S(2)}, u32[]{:S(2)}) collective-permute-start(bf16[160,3584]{1,0:T(8,128)(2,1)} %get-tuple-element.37), channel_id=1, source_target_pairs={{0,2},{1,3},{2,0},{3,1},{4,6},{5,7},{6,4},{7,5},{8,10},{9,11},{10,... | collective-permute-start | bytes 3440648 | tf_op jit(solution)/shard_map/ppermute | solution.py:113
  246.2 34.9 %collective-permute-start.17 = (bf16[288,1024]{1,0:T(8,128)(2,1)S(1)}, bf16[288,1024]{1,0:T(8,128)(2,1)S(1)}, u32[]{:S(2)}, u32[]{:S(2)}) collective-permute-start(bf16[288,1024]{1,0:T(8,128)(2,1)S(1)} %get-tuple-element.52), channel_id=1, source_target_pairs={{0,2},{1,3},{2,0},{3,1},{4,6},{5,7},{6,4},{7,5},{8,10},{9,11},{10,... | collective-permute-start | bytes 1769480 | tf_op jit(solution)/shard_map/ppermute | solution.py:113
  246.3 48.7 %collective-permute-start.18 = (bf16[288,1024]{1,0:T(8,128)(2,1)}, bf16[288,1024]{1,0:T(8,128)(2,1)S(1)}, u32[]{:S(2)}, u32[]{:S(2)}) collective-permute-start(bf16[288,1024]{1,0:T(8,128)(2,1)} %get-tuple-element.51), channel_id=1, source_target_pairs={{0,3},{1,2},{2,1},{3,0},{4,7},{5,6},{6,5},{7,4},{8,11},{9,10},{10,... | collective-permute-start | bytes 1769480 | tf_op jit(solution)/shard_map/ppermute | solution.py:113
  247.9 47.2 %collective-permute-start.19 = (bf16[64,3584]{1,0:T(8,128)(2,1)}, bf16[64,3584]{1,0:T(8,128)(2,1)S(1)}, u32[]{:S(2)}, u32[]{:S(2)}) collective-permute-start(bf16[64,3584]{1,0:T(8,128)(2,1)} %get-tuple-element.63), channel_id=1, source_target_pairs={{0,1},{1,0},{2,3},{3,2},{4,5},{5,4},{6,7},{7,6},{8,9},{9,8},{10,11... | collective-permute-start | bytes 1376264 | tf_op jit(solution)/shard_map/ppermute | solution.py:113
  248.1 55.5 %collective-permute-start.20 = (bf16[64,3584]{1,0:T(8,128)(2,1)}, bf16[64,3584]{1,0:T(8,128)(2,1)S(1)}, u32[]{:S(2)}, u32[]{:S(2)}) collective-permute-start(bf16[64,3584]{1,0:T(8,128)(2,1)} %get-tuple-element.62), channel_id=1, source_target_pairs={{0,2},{1,3},{2,0},{3,1},{4,6},{5,7},{6,4},{7,5},{8,10},{9,11},{10,... | collective-permute-start | bytes 1376264 | tf_op jit(solution)/shard_map/ppermute | solution.py:113
  281.9 32.0 %collective-permute-start.21 = (bf16[64,3584]{1,0:T(8,128)(2,1)S(1)}, bf16[64,3584]{1,0:T(8,128)(2,1)S(1)}, u32[]{:S(2)}, u32[]{:S(2)}) collective-permute-start(bf16[64,3584]{1,0:T(8,128)(2,1)S(1)} %copy-done.29), channel_id=1, source_target_pairs={{0,3},{1,2},{2,1},{3,0},{4,7},{5,6},{6,5},{7,4},{8,11},{9,10},{10,... | collective-permute-start | bytes 1376264 | tf_op jit(solution)/shard_map/ppermute | solution.py:113
  330.7 37.2 %collective-permute-start.24 = (bf16[48,3584]{1,0:T(8,128)(2,1)S(1)}, bf16[48,3584]{1,0:T(8,128)(2,1)S(1)}, u32[]{:S(2)}, u32[]{:S(2)}) collective-permute-start(bf16[48,3584]{1,0:T(8,128)(2,1)S(1)} %get-tuple-element.67), channel_id=1, source_target_pairs={{0,1},{1,0},{2,3},{3,2},{4,5},{5,4},{6,7},{7,6},{8,9},{9,8},{10,11... | collective-permute-start | bytes 1032200 | tf_op jit(solution)/shard_map/ppermute | solution.py:113
  331.2 36.7 %collective-permute-start.25 = (bf16[48,3584]{1,0:T(8,128)(2,1)S(1)}, bf16[48,3584]{1,0:T(8,128)(2,1)S(1)}, u32[]{:S(2)}, u32[]{:S(2)}) collective-permute-start(bf16[48,3584]{1,0:T(8,128)(2,1)S(1)} %get-tuple-element.66), channel_id=1, source_target_pairs={{0,2},{1,3},{2,0},{3,1},{4,6},{5,7},{6,4},{7,5},{8,10},{9,11},{10,... | collective-permute-start | bytes 1032200 | tf_op jit(solution)/shard_map/ppermute | solution.py:113
  332.6 35.3 %collective-permute-start.26 = (bf16[48,3584]{1,0:T(8,128)(2,1)S(1)}, bf16[48,3584]{1,0:T(8,128)(2,1)S(1)}, u32[]{:S(2)}, u32[]{:S(2)}) collective-permute-start(bf16[48,3584]{1,0:T(8,128)(2,1)S(1)} %get-tuple-element.65), channel_id=1, source_target_pairs={{0,3},{1,2},{2,1},{3,0},{4,7},{5,6},{6,5},{7,4},{8,11},{9,10},{10,... | collective-permute-start | bytes 1032200 | tf_op jit(solution)/shard_map/ppermute | solution.py:113
  333.4 34.4 %collective-permute-start.23 = (bf16[128,3584]{1,0:T(8,128)(2,1)S(1)}, bf16[128,3584]{1,0:T(8,128)(2,1)S(1)}, u32[]{:S(2)}, u32[]{:S(2)}) collective-permute-start(bf16[128,3584]{1,0:T(8,128)(2,1)S(1)} %get-tuple-element.35), channel_id=1, source_target_pairs={{0,2},{1,3},{2,0},{3,1},{4,6},{5,7},{6,4},{7,5},{8,10},{9,11},{10,... | collective-permute-start | bytes 2752520 | tf_op jit(solution)/shard_map/ppermute | solution.py:113
  336.7 70.9 %collective-permute-start.29 = (bf16[192,3584]{1,0:T(8,128)(2,1)S(1)}, bf16[192,3584]{1,0:T(8,128)(2,1)S(1)}, u32[]{:S(2)}, u32[]{:S(2)}) collective-permute-start(bf16[192,3584]{1,0:T(8,128)(2,1)S(1)} %pad_maximum_fusion.1.refs_0_), channel_id=1, source_target_pairs={{0,1},{1,0},{2,3},{3,2},{4,5},{5,4},{6,7},{7,6},{8,9},{9,8},{10,11... | collective-permute-start | bytes 4128776 | tf_op jit(solution)/shard_map/ppermute | solution.py:113
  386.1 21.4 %collective-permute-start.30 = (bf16[160,3584]{1,0:T(8,128)(2,1)S(1)}, bf16[160,3584]{1,0:T(8,128)(2,1)S(1)}, u32[]{:S(2)}, u32[]{:S(2)}) collective-permute-start(bf16[160,3584]{1,0:T(8,128)(2,1)S(1)} %pad_maximum_fusion.2.refs_1_), channel_id=1, source_target_pairs={{0,1},{1,0},{2,3},{3,2},{4,5},{5,4},{6,7},{7,6},{8,9},{9,8},{10,11... | collective-permute-start | bytes 3440648 | tf_op jit(solution)/shard_map/ppermute | solution.py:113
  387.1 17.0 %collective-permute-start.28 = (bf16[96,3584]{1,0:T(8,128)(2,1)S(1)}, bf16[96,3584]{1,0:T(8,128)(2,1)S(1)}, u32[]{:S(2)}, u32[]{:S(2)}) collective-permute-start(bf16[96,3584]{1,0:T(8,128)(2,1)S(1)} %get-tuple-element.33), channel_id=1, source_target_pairs={{0,2},{1,3},{2,0},{3,1},{4,6},{5,7},{6,4},{7,5},{8,10},{9,11},{10,... | collective-permute-start | bytes 2064392 | tf_op jit(solution)/shard_map/ppermute | solution.py:113
  388.8 18.8 %collective-permute-start.31 = (bf16[128,3584]{1,0:T(8,128)(2,1)S(1)}, bf16[128,3584]{1,0:T(8,128)(2,1)S(1)}, u32[]{:S(2)}, u32[]{:S(2)}) collective-permute-start(bf16[128,3584]{1,0:T(8,128)(2,1)S(1)} %pad_maximum_fusion.3.refs_2_), channel_id=1, source_target_pairs={{0,1},{1,0},{2,3},{3,2},{4,5},{5,4},{6,7},{7,6},{8,9},{9,8},{10,11... | collective-permute-start | bytes 2752520 | tf_op jit(solution)/shard_map/ppermute | solution.py:113
  404.4 4.3 collective-permute-start.32
  (36 other events, 345.5 us)
Sparse Core Ops, SparseCore 0:
  8.9 58.1 all-gather.4
  68.7 48.1 all-gather.6
  123.2 80.2 all-gather.8
  237.3 33.3 all-gather.10
